TPU v7x, 256 devices: a whole 4x4x8 slice. The times are simulated.
256 devices in a mesh: pipe: 8 (over x, core), expert: 32 (over z, y).
Axes of the slice: x: 4, y: 4, z: 8, core: 2. Of those that a mesh axis runs over, the one named last changes fastest.
Arguments:
- layer_input: bfloat16 [8, 8192, 3584], P('pipe', 'expert'), may hold values from -6 to 6
- out_grad: bfloat16 [8, 8192, 3584], P('pipe', 'expert'), may hold values from -6 to 6
- combine_weights: float32 [8, 8192, 8], P('pipe', 'expert'), may hold values from 0.05 to 1
- expert_ids: int32 [8, 8192, 8], P('pipe', 'expert'), may hold values from 0 to 255, as said below
- w_gate: bfloat16 [8, 3584, 4096], P('pipe', None, 'expert'), as said below
- w_up: bfloat16 [8, 3584, 4096], P('pipe', None, 'expert'), as said below
- w_down: bfloat16 [8, 4096, 3584], P('pipe', 'expert'), as said below
Outputs:
- input_grad: bfloat16 [8, 8192, 3584], P('pipe', 'expert')
- gate_grad: bfloat16 [8, 3584, 4096], P('pipe', None, 'expert')
- up_grad: bfloat16 [8, 3584, 4096], P('pipe', None, 'expert')
- down_grad: bfloat16 [8, 4096, 3584], P('pipe', 'expert')
Inputs may be any that keep to these rules, and one draw needn't show every extreme that they name: `expert_ids`: each row names 8 different experts. Among the tokens of one device (one section, one aligned block of 256) each expert below 4 is named by 1 to 16 tokens; in each section one of these experts is named by exactly 16 tokens on every device. w_gate[p] equals w_gate[7 - p]. w_up[p] equals w_up[7 - p]. w_down[p] equals w_down[7 - p].
All inputs are finite; a program needn't handle non-finite values.
Results may differ from a plain program's by a relative error of at most 0.02.
Values may be sent and summed in bfloat16 or wider, within the bound.
A program may use at most 128 MiB of HBM per device.

v0:
```python
import jax
import jax.numpy as jnp
from jax import lax
from jax.sharding import PartitionSpec as P

SPLIT = 8
CAP = 16


def partner_2(shard, axis, bit):
    return lax.ppermute(shard, axis, [(i, i ^ 1 << bit) for i in range(lax.axis_size(axis))])


def body(layer_input, out_grad, combine_weights, expert_ids, w_gate, w_up, w_down):
    experts_total = lax.axis_size("expert")
    sections = lax.axis_size("pipe")
    tokens_here = layer_input.shape[1]
    width = layer_input.shape[2]
    flight = experts_total // SPLIT
    capacity = CAP
    slot_rows = experts_total * capacity
    own_ids = expert_ids[0]
    own_probs = combine_weights[0]
    numbers = jnp.arange(flight, dtype=jnp.int32)
    chosen = own_ids[:, :, None] == numbers[None, None, :]
    selected = jnp.any(chosen, axis=1).astype(jnp.int32)
    weight_sel = jnp.sum(jnp.where(chosen, own_probs[:, :, None], jnp.float32(0.0)), axis=1)
    slots = jnp.cumsum(selected, axis=0) - selected
    placed = (selected.T[:, None, :] == 1) & (
        slots.T[:, None, :] == jnp.arange(capacity, dtype=jnp.int32)[None, :, None]
    )
    place_float = placed.astype(jnp.float32)
    place_matrix = placed.reshape(flight * capacity, tokens_here).astype(jnp.bfloat16)
    sent_input = jnp.dot(place_matrix, layer_input[0], preferred_element_type=jnp.float32).astype(
        jnp.bfloat16
    )
    sent_grad = jnp.dot(place_matrix, out_grad[0], preferred_element_type=jnp.float32).astype(
        jnp.bfloat16
    )
    sent_scale = jnp.sum(place_float * weight_sel.T[:, None, :], axis=2)
    copies_input = jnp.repeat(sent_input.reshape(flight, capacity, width), SPLIT, axis=0)
    copies_grad = jnp.repeat(sent_grad.reshape(flight, capacity, width), SPLIT, axis=0)
    copies_scale = jnp.repeat(sent_scale, SPLIT, axis=0)
    got_input, got_grad, got_scale = (
        lax.all_to_all(copies_input, "expert", split_axis=0, concat_axis=0, tiled=True),
        lax.all_to_all(copies_grad, "expert", split_axis=0, concat_axis=0, tiled=True),
        lax.all_to_all(
            copies_scale.astype(jnp.bfloat16), "expert", split_axis=0, concat_axis=0, tiled=True
        ).astype(copies_scale.dtype),
    )
    rows_input = got_input.reshape(slot_rows, width)
    rows_grad = got_grad.reshape(slot_rows, width)
    scaled = (got_scale.reshape(slot_rows, 1) * rows_grad.astype(jnp.float32)).astype(jnp.bfloat16)
    gate_local = w_gate[0]
    up_local = w_up[0]
    down_local = w_down[0]
    pre_gate = jnp.dot(rows_input, gate_local, preferred_element_type=jnp.float32)
    pre_up = jnp.dot(rows_input, up_local, preferred_element_type=jnp.float32)
    sigmoid_gate = jax.nn.sigmoid(pre_gate)
    activated = pre_gate * sigmoid_gate
    hidden = (activated * pre_up).astype(jnp.bfloat16)
    last_pair = (((1,), (1,)), ((), ()))
    first_pair = (((0,), (0,)), ((), ()))
    d_hidden = lax.dot_general(scaled, down_local, last_pair, preferred_element_type=jnp.float32)
    d_gate = (d_hidden * pre_up * sigmoid_gate * (1.0 + pre_gate * (1.0 - sigmoid_gate))).astype(
        jnp.bfloat16
    )
    d_up = (d_hidden * activated).astype(jnp.bfloat16)
    grad_down = lax.dot_general(
        hidden, scaled, first_pair, preferred_element_type=jnp.float32
    ).astype(jnp.bfloat16)
    grad_gate = lax.dot_general(
        rows_input, d_gate, first_pair, preferred_element_type=jnp.float32
    ).astype(jnp.bfloat16)
    grad_up = lax.dot_general(
        rows_input, d_up, first_pair, preferred_element_type=jnp.float32
    ).astype(jnp.bfloat16)
    partial_value = lax.dot_general(
        d_gate, gate_local, last_pair, preferred_element_type=jnp.float32
    )
    partial_value = (
        partial_value
        + lax.dot_general(d_up, up_local, last_pair, preferred_element_type=jnp.float32)
    ).astype(jnp.bfloat16)
    returned = lax.all_to_all(
        partial_value.reshape(experts_total, capacity, width),
        "expert",
        split_axis=0,
        concat_axis=0,
        tiled=True,
    )
    summed = jnp.sum(returned.reshape(flight, SPLIT, capacity, width).astype(jnp.float32), axis=1)
    token_grad = jnp.einsum("ect,ecd->td", place_float, summed, precision=lax.Precision.HIGHEST)
    input_grad = token_grad.astype(jnp.bfloat16)[None]
    section_grads = (grad_gate, grad_up, grad_down)
    partner = section_grads
    for bit_index in range(sections.bit_length() - 1):
        partner = partner_2((partner[0], partner[1], partner[2]), "pipe", bit_index)
    totals = tuple(
        (
            (own_term.astype(jnp.float32) + mirror_term.astype(jnp.float32)).astype(jnp.bfloat16)
            for own_term, mirror_term in zip(section_grads, partner)
        )
    )
    return (input_grad, totals[0][None], totals[1][None], totals[2][None])


def solution(mesh):
    return jax.shard_map(
        body,
        mesh=mesh,
        in_specs=(
            P("pipe", "expert", None),
            P("pipe", "expert", None),
            P("pipe", "expert", None),
            P("pipe", "expert", None),
            P("pipe", None, "expert"),
            P("pipe", None, "expert"),
            P("pipe", "expert", None),
        ),
        out_specs=(
            P("pipe", "expert", None),
            P("pipe", None, "expert"),
            P("pipe", None, "expert"),
            P("pipe", "expert", None),
        ),
        check_vma=False,
    )
```

profile of v0, /device:TPU:1, one launch (start us, length us, event | category | flops | bytes accessed | tf_op | source)
XLA Modules:
  0.0 364.2 jit_solution(16399905277070341274)
XLA Ops:
  1.5 1.2 reduce-window.6
  4.6 12.0 %all-to-all-start = ((bf16[32,1,16]{2,1,0:T(2,128)(2,1)}), bf16[32,1,16]{2,1,0:T(2,128)(2,1)S(1)}, u32[]{:S(2)}, u32[]{:S(2)}) async-start(bf16[32,1,16]{2,1,0:T(2,128)(2,1)} %copy.30), calls=%async_computation | async-start | bytes 32768 | tf_op jit(solution)/shard_map/all_to_all | solution.py:47
  17.1 8.0 %all-to-all-done = bf16[32,1,16]{2,1,0:T(2,128)(2,1)S(1)} async-done(((bf16[32,1,16]{2,1,0:T(2,128)(2,1)}), bf16[32,1,16]{2,1,0:T(2,128)(2,1)S(1)}, u32[]{:S(2)}, u32[]{:S(2)}) %all-to-all-start) | async-done | bytes 1056 | tf_op jit(solution)/shard_map/all_to_all | solution.py:47
  25.2 2.3 broadcast_in_dim.45
  27.4 4.8 %all-to-all-start.2 = ((bf16[32,16,3584]{2,1,0:T(8,128)(2,1)}), bf16[32,16,3584]{2,1,0:T(8,128)(2,1)}, u32[]{:S(2)}, u32[]{:S(2)}) async-start(bf16[32,16,3584]{2,1,0:T(8,128)(2,1)} %bitcast.82), calls=%async_computation.2 | async-start | bytes 7340032 | tf_op jit(solution)/shard_map/all_to_all | solution.py:45
  32.3 1.9 convolution_convert_fusion.4
  34.2 80.0 %all-to-all-done.2 = bf16[32,16,3584]{2,1,0:T(8,128)(2,1)} async-done(((bf16[32,16,3584]{2,1,0:T(8,128)(2,1)}), bf16[32,16,3584]{2,1,0:T(8,128)(2,1)}, u32[]{:S(2)}, u32[]{:S(2)}) %all-to-all-start.2) | async-done | bytes 3670048 | tf_op jit(solution)/shard_map/all_to_all | solution.py:45
  114.2 2.3 broadcast_in_dim.44
  116.6 7.4 %all-to-all-start.1 = ((bf16[32,16,3584]{2,1,0:T(8,128)(2,1)}), bf16[32,16,3584]{2,1,0:T(8,128)(2,1)}, u32[]{:S(2)}, u32[]{:S(2)}) async-start(bf16[32,16,3584]{2,1,0:T(8,128)(2,1)} %bitcast.81), calls=%async_computation.1 | async-start | bytes 7340032 | tf_op jit(solution)/shard_map/all_to_all | solution.py:46
  124.2 3.2 fusion.10
  127.4 3.1 fusion.13
  130.5 75.2 %all-to-all-done.1 = bf16[32,16,3584]{2,1,0:T(8,128)(2,1)} async-done(((bf16[32,16,3584]{2,1,0:T(8,128)(2,1)}), bf16[32,16,3584]{2,1,0:T(8,128)(2,1)}, u32[]{:S(2)}, u32[]{:S(2)}) %all-to-all-start.1) | async-done | bytes 3670048 | tf_op jit(solution)/shard_map/all_to_all | solution.py:46
  205.8 3.2 multiply_convert_fusion
  211.3 3.0 add_convert_fusion
  214.4 6.8 %all-to-all-start.3 = ((bf16[32,16,3584]{2,1,0:T(8,128)(2,1)}), bf16[32,16,3584]{2,1,0:T(8,128)(2,1)}, u32[]{:S(2)}, u32[]{:S(2)}) async-start(bf16[32,16,3584]{2,1,0:T(8,128)(2,1)} %bitcast.80), calls=%async_computation.3 | async-start | bytes 7340032 | tf_op jit(solution)/shard_map/all_to_all | solution.py:85
  221.1 3.1 fusion
  224.9 2.8 collective-permute-start.6
  227.7 3.2 convolution_convert_fusion.1
  231.2 3.2 convolution_convert_fusion.2
  235.0 1.2 collective-permute-start.7
  237.1 1.2 collective-permute-start.1
  238.4 18.7 %collective-permute-done.7 = bf16[128,3584]{1,0:T(8,128)(2,1)S(1)} collective-permute-done((bf16[128,3584]{1,0:T(8,128)(2,1)S(1)}, bf16[128,3584]{1,0:T(8,128)(2,1)S(1)}, u32[]{:S(2)}, u32[]{:S(2)}) %collective-permute-start.7) | collective-permute-done | bytes 917536 | tf_op jit(solution)/shard_map/ppermute | solution.py:11
  257.1 2.7 collective-permute-start.8
  259.8 16.9 %collective-permute-done.4 = bf16[3584,128]{1,0:T(8,128)(2,1)S(1)} collective-permute-done((bf16[3584,128]{1,0:T(8,128)(2,1)S(1)}, bf16[3584,128]{1,0:T(8,128)(2,1)S(1)}, u32[]{:S(2)}, u32[]{:S(2)}) %collective-permute-start.4) | collective-permute-done | bytes 917536 | tf_op jit(solution)/shard_map/ppermute | solution.py:11
  276.7 2.7 collective-permute-start.5
  279.5 16.9 %collective-permute-done.1 = bf16[3584,128]{1,0:T(8,128)(2,1)S(1)} collective-permute-done((bf16[3584,128]{1,0:T(8,128)(2,1)S(1)}, bf16[3584,128]{1,0:T(8,128)(2,1)S(1)}, u32[]{:S(2)}, u32[]{:S(2)}) %collective-permute-start.1) | collective-permute-done | bytes 917536 | tf_op jit(solution)/shard_map/ppermute | solution.py:11
  296.4 2.7 collective-permute-start.2
  299.1 19.0 %collective-permute-done.8 = bf16[128,3584]{1,0:T(8,128)(2,1)S(1)} collective-permute-done((bf16[128,3584]{1,0:T(8,128)(2,1)S(1)}, bf16[128,3584]{1,0:T(8,128)(2,1)S(1)}, u32[]{:S(2)}, u32[]{:S(2)}) %collective-permute-start.8) | collective-permute-done | bytes 917536 | tf_op jit(solution)/shard_map/ppermute | solution.py:11
  319.3 18.5 %collective-permute-done.5 = bf16[3584,128]{1,0:T(8,128)(2,1)S(1)} collective-permute-done((bf16[3584,128]{1,0:T(8,128)(2,1)S(1)}, bf16[3584,128]{1,0:T(8,128)(2,1)S(1)}, u32[]{:S(2)}, u32[]{:S(2)}) %collective-permute-start.5) | collective-permute-done | bytes 917536 | tf_op jit(solution)/shard_map/ppermute | solution.py:11
  339.0 18.5 %collective-permute-done.2 = bf16[3584,128]{1,0:T(8,128)(2,1)S(1)} collective-permute-done((bf16[3584,128]{1,0:T(8,128)(2,1)S(1)}, bf16[3584,128]{1,0:T(8,128)(2,1)S(1)}, u32[]{:S(2)}, u32[]{:S(2)}) %collective-permute-start.2) | collective-permute-done | bytes 917536 | tf_op jit(solution)/shard_map/ppermute | solution.py:11
  358.6 2.6 convert_reduce_fusion
  361.3 2.9 fusion.2
  (43 shorter events, 11.5 us)
Async XLA Ops:
  0.6 16.1 %copy-start = (bf16[1,256,3584]{2,1,0:T(8,128)(2,1)S(1)}, bf16[1,256,3584]{2,1,0:T(8,128)(2,1)}, u32[]{:S(2)}) copy-start(bf16[1,256,3584]{2,1,0:T(8,128)(2,1)} %param.7) | copy-start | bytes 5505028
  4.6 20.5 %all-to-all-start = ((bf16[32,1,16]{2,1,0:T(2,128)(2,1)}), bf16[32,1,16]{2,1,0:T(2,128)(2,1)S(1)}, u32[]{:S(2)}, u32[]{:S(2)}) async-start(bf16[32,1,16]{2,1,0:T(2,128)(2,1)} %copy.30), calls=%async_computation | async-start | bytes 32768 | tf_op jit(solution)/shard_map/all_to_all | solution.py:47
  27.4 86.8 %all-to-all-start.2 = ((bf16[32,16,3584]{2,1,0:T(8,128)(2,1)}), bf16[32,16,3584]{2,1,0:T(8,128)(2,1)}, u32[]{:S(2)}, u32[]{:S(2)}) async-start(bf16[32,16,3584]{2,1,0:T(8,128)(2,1)} %bitcast.82), calls=%async_computation.2 | async-start | bytes 7340032 | tf_op jit(solution)/shard_map/all_to_all | solution.py:45
  116.6 7.6 %copy-start.1 = (bf16[1,3584,128]{2,1,0:T(8,128)(2,1)S(1)}, bf16[1,3584,128]{2,1,0:T(8,128)(2,1)}, u32[]{:S(2)}) copy-start(bf16[1,3584,128]{2,1,0:T(8,128)(2,1)} %param.11) | copy-start | bytes 2752516
  116.6 89.2 %all-to-all-start.1 = ((bf16[32,16,3584]{2,1,0:T(8,128)(2,1)}), bf16[32,16,3584]{2,1,0:T(8,128)(2,1)}, u32[]{:S(2)}, u32[]{:S(2)}) async-start(bf16[32,16,3584]{2,1,0:T(8,128)(2,1)} %bitcast.81), calls=%async_computation.1 | async-start | bytes 7340032 | tf_op jit(solution)/shard_map/all_to_all | solution.py:46
  124.1 3.3 copy-start.2
  205.8 3.3 copy-start.4
  210.2 1.2 copy-start.3
  214.4 144.3 %all-to-all-start.3 = ((bf16[32,16,3584]{2,1,0:T(8,128)(2,1)}), bf16[32,16,3584]{2,1,0:T(8,128)(2,1)}, u32[]{:S(2)}, u32[]{:S(2)}) async-start(bf16[32,16,3584]{2,1,0:T(8,128)(2,1)} %bitcast.80), calls=%async_computation.3 | async-start | bytes 7340032 | tf_op jit(solution)/shard_map/all_to_all | solution.py:85
  224.9 10.1 %collective-permute-start.6 = (bf16[128,3584]{1,0:T(8,128)(2,1)S(1)}, bf16[128,3584]{1,0:T(8,128)(2,1)S(1)}, u32[]{:S(2)}, u32[]{:S(2)}) collective-permute-start(bf16[128,3584]{1,0:T(8,128)(2,1)S(1)} %convolution_convert_fusion), channel_id=1, source_target_pairs={{0,32},{32,0},{64,96},{96,64},{128,160},{160,128},{192,224},{224,1... | collective-permute-start | bytes 2752520 | tf_op jit(solution)/shard_map/ppermute | solution.py:11
  231.0 5.3 %collective-permute-start.3 = (bf16[3584,128]{1,0:T(8,128)(2,1)S(1)}, bf16[3584,128]{1,0:T(8,128)(2,1)S(1)}, u32[]{:S(2)}, u32[]{:S(2)}) collective-permute-start(bf16[3584,128]{1,0:T(8,128)(2,1)S(1)} %convolution_convert_fusion.1), channel_id=1, source_target_pairs={{0,32},{32,0},{64,96},{96,64},{128,160},{160,128},{192,224},{224,1... | collective-permute-start | bytes 2752520 | tf_op jit(solution)/shard_map/ppermute | solution.py:11
  234.5 2.7 collective-permute-start
  235.0 22.0 %collective-permute-start.7 = (bf16[128,3584]{1,0:T(8,128)(2,1)S(1)}, bf16[128,3584]{1,0:T(8,128)(2,1)S(1)}, u32[]{:S(2)}, u32[]{:S(2)}) collective-permute-start(bf16[128,3584]{1,0:T(8,128)(2,1)S(1)} %collective-permute-done.6), channel_id=1, source_target_pairs={{0,64},{32,96},{64,0},{96,32},{128,192},{160,224},{192,128},{224,1... | collective-permute-start | bytes 2752520 | tf_op jit(solution)/shard_map/ppermute | solution.py:11
  236.3 40.4 %collective-permute-start.4 = (bf16[3584,128]{1,0:T(8,128)(2,1)S(1)}, bf16[3584,128]{1,0:T(8,128)(2,1)S(1)}, u32[]{:S(2)}, u32[]{:S(2)}) collective-permute-start(bf16[3584,128]{1,0:T(8,128)(2,1)S(1)} %collective-permute-done.3), channel_id=1, source_target_pairs={{0,64},{32,96},{64,0},{96,32},{128,192},{160,224},{192,128},{224,1... | collective-permute-start | bytes 2752520 | tf_op jit(solution)/shard_map/ppermute | solution.py:11
  237.1 59.3 %collective-permute-start.1 = (bf16[3584,128]{1,0:T(8,128)(2,1)S(1)}, bf16[3584,128]{1,0:T(8,128)(2,1)S(1)}, u32[]{:S(2)}, u32[]{:S(2)}) collective-permute-start(bf16[3584,128]{1,0:T(8,128)(2,1)S(1)} %collective-permute-done), channel_id=1, source_target_pairs={{0,64},{32,96},{64,0},{96,32},{128,192},{160,224},{192,128},{224,1... | collective-permute-start | bytes 2752520 | tf_op jit(solution)/shard_map/ppermute | solution.py:11
  257.1 61.1 %collective-permute-start.8 = (bf16[128,3584]{1,0:T(8,128)(2,1)S(1)}, bf16[128,3584]{1,0:T(8,128)(2,1)S(1)}, u32[]{:S(2)}, u32[]{:S(2)}) collective-permute-start(bf16[128,3584]{1,0:T(8,128)(2,1)S(1)} %collective-permute-done.7), channel_id=1, source_target_pairs={{0,128},{32,160},{64,192},{96,224},{128,0},{160,32},{192,64},{224,... | collective-permute-start | bytes 2752520 | tf_op jit(solution)/shard_map/ppermute | solution.py:11
  276.7 61.1 %collective-permute-start.5 = (bf16[3584,128]{1,0:T(8,128)(2,1)S(1)}, bf16[3584,128]{1,0:T(8,128)(2,1)S(1)}, u32[]{:S(2)}, u32[]{:S(2)}) collective-permute-start(bf16[3584,128]{1,0:T(8,128)(2,1)S(1)} %collective-permute-done.4), channel_id=1, source_target_pairs={{0,128},{32,160},{64,192},{96,224},{128,0},{160,32},{192,64},{224,... | collective-permute-start | bytes 2752520 | tf_op jit(solution)/shard_map/ppermute | solution.py:11
  296.4 61.1 %collective-permute-start.2 = (bf16[3584,128]{1,0:T(8,128)(2,1)S(1)}, bf16[3584,128]{1,0:T(8,128)(2,1)S(1)}, u32[]{:S(2)}, u32[]{:S(2)}) collective-permute-start(bf16[3584,128]{1,0:T(8,128)(2,1)S(1)} %collective-permute-done.1), channel_id=1, source_target_pairs={{0,128},{32,160},{64,192},{96,224},{128,0},{160,32},{192,64},{224,... | collective-permute-start | bytes 2752520 | tf_op jit(solution)/shard_map/ppermute | solution.py:11
where the time goes:
time: 365 us; the launch traced here: 364 us
  waiting for transfers between devices  273 us (75%)
  starting transfers between devices  45.6 us (12%)
  matrix products  24 us (7%)
  other arithmetic  15.5 us (4%)
  local copies, waits for them, and re-layouts  5.66 us (2%)
    ppermute x9, waiting for transfers between devices, partner_2(): lax.ppermute(shard, axis, [(i, i ^ 1 << bit) for i in range(lax.axis_size...  109 us
    all_to_all x1, waiting for transfers between devices, body(): lax.all_to_all(copies_input, 'expert', split_axis=0, concat_axis=0, tiled...  80 us
    all_to_all x1, waiting for transfers between devices, body(): lax.all_to_all(copies_grad, 'expert', split_axis=0, concat_axis=0, tiled=...  75.2 us
    ppermute x9, starting transfers between devices, partner_2(): lax.ppermute(shard, axis, [(i, i ^ 1 << bit) for i in range(lax.axis_size...  14.6 us
    all_to_all x1, starting transfers between devices, body(): lax.all_to_all(copies_scale.astype(jnp.bfloat16), 'expert', split_axis=0,...  12 us
    all_to_all x1, waiting for transfers between devices, body(): lax.all_to_all(copies_scale.astype(jnp.bfloat16), 'expert', split_axis=0,...  8.03 us
    all_to_all x1, starting transfers between devices, body(): lax.all_to_all(copies_grad, 'expert', split_axis=0, concat_axis=0, tiled=...  7.4 us
  transfers between devices with their start and end apart: 13, of which 10 were waited for; matrix products, arithmetic and copies ran while one was open for 6% of the time, Pallas kernels for 0%

commit v1 on v0

v1 whole, which is shorter than its diff:
```python
import jax
import jax.numpy as jnp
from jax import lax
from jax.experimental import pallas as pl
from jax.experimental.pallas import tpu as pltpu
from jax.sharding import PartitionSpec as P

MESH = pl.DeviceIdType.MESH
BF16 = jnp.bfloat16
F32 = jnp.float32

NY = 4
NZ = 8
EF = 4
CAP = 16
DELTA = (0, 1, 7, 2, 6, 3, 5, 4)
COLS = 256
ANY = pl.BlockSpec(memory_space=pl.ANY)
VMEM = pl.BlockSpec(memory_space=pltpu.VMEM)


def dot(a, b):
    return jnp.dot(a, b, preferred_element_type=F32)


def kernel(
    ids,
    probs,
    x_h,
    g_h,
    wg_h,
    wu_h,
    wd_h,
    ig_h,
    gg_h,
    ug_h,
    dg_h,
    tok,
    wgu,
    wd,
    wgut,
    wdt,
    pmat,
    pmat_t,
    wslot,
    s_own,
    s_mir,
    s_out,
    rows,
    pf,
    ps,
    pr,
    da,
    dat,
    go_g,
    go_u,
    go_d,
    pb,
    anti,
    near,
    fin,
    home,
    slots,
    slots_m,
    slots_o,
    out,
    lsem,
    bsem,
    zs,
    zr,
    ys,
    yr,
    fs,
    fr,
    xs,
    xr,
    cs,
    ans,
    anr,
    ns,
    nr,
    hs,
    hr,
    gs,
    gr,
    gl,
    ol,
):
    n_pipe = lax.axis_size("pipe")
    p = lax.axis_index("pipe")
    ex = lax.axis_index("expert")
    z = lax.div(ex, NY)
    y = lax.rem(ex, NY)
    tokens, half_width = tok.shape[1], tok.shape[2]
    n_cols = half_width // COLS
    half = lax.div(p, n_pipe // 2)
    col = pl.multiple_of(half * half_width, 128)
    ocol = pl.multiple_of((1 - half) * half_width, 128)
    mirror = (n_pipe - 1 - p, ex)
    y_up = (p, z * NY + lax.rem(y + 1, NY))
    y_dn = (p, z * NY + lax.rem(y + NY - 1, NY))

    def z_at(delta):
        return (p, lax.rem(z + delta, NZ) * NY + y)

    def remote(src, dst, send, recv, device):
        return pltpu.make_async_remote_copy(
            src_ref=src, dst_ref=dst, send_sem=send, recv_sem=recv, device_id=device, device_id_type=MESH
        )

    def cut(n):
        return pl.ds(pl.multiple_of(n * COLS, COLS), COLS)

    loads = [
        pltpu.make_async_copy(x_h.at[:, pl.ds(col, half_width)], tok.at[0], lsem.at[0]),
        pltpu.make_async_copy(g_h.at[:, pl.ds(col, half_width)], tok.at[1], lsem.at[1]),
        pltpu.make_async_copy(x_h.at[:, pl.ds(ocol, half_width)], tok.at[2], lsem.at[2]),
        pltpu.make_async_copy(g_h.at[:, pl.ds(ocol, half_width)], tok.at[3], lsem.at[3]),
        pltpu.make_async_copy(wg_h.at[pl.ds(col, half_width), :], wgu.at[:, pl.ds(0, 128)], lsem.at[4]),
        pltpu.make_async_copy(wu_h.at[pl.ds(col, half_width), :], wgu.at[:, pl.ds(128, 128)], lsem.at[5]),
        pltpu.make_async_copy(wd_h.at[:, pl.ds(col, half_width)], wd, lsem.at[6]),
    ]
    for c in loads:
        c.start()

    barrier = pltpu.get_barrier_semaphore()
    partners = [mirror, y_up, y_dn] + [z_at(d) for d in range(1, NZ)]
    for device in partners:
        pl.semaphore_signal(barrier, inc=1, device_id=device, device_id_type=MESH)

    lane = lax.broadcasted_iota(jnp.int32, (tokens, 128), 1)
    lane_expert = lax.div(lane, CAP)
    named = jnp.zeros((tokens, 128), F32)
    weight = jnp.zeros((tokens, 128), F32)
    for k in range(ids.shape[1]):
        hit = ids[:, k : k + 1] == lane_expert
        named = jnp.where(hit, 1.0, named)
        weight = jnp.where(hit, probs[:, k : k + 1], weight)
    named = jnp.where(lane < EF * CAP, named, 0.0)
    before = (
        lax.broadcasted_iota(jnp.int32, (tokens, tokens), 0) > lax.broadcasted_iota(jnp.int32, (tokens, tokens), 1)
    ).astype(F32)
    count = dot(before.astype(BF16), named.astype(BF16))
    placed = jnp.where(count == lax.rem(lane, CAP).astype(F32), named, 0.0)
    pmat_t[...] = placed.astype(BF16)
    pmat[...] = placed.T.astype(BF16)
    wslot[...] = jnp.sum((placed * weight).T, axis=1, keepdims=True)

    def gather(base, dst):
        def step(n, _):
            x_rows = dot(pmat[0 : EF * CAP, :], tok[base, :, cut(n)])
            dst[0, :, :, cut(n)] = x_rows.astype(BF16).reshape(EF, CAP, COLS)
            g_rows = dot(pmat[0 : EF * CAP, :], tok[base + 1, :, cut(n)]) * wslot[0 : EF * CAP, :]
            dst[1, :, :, cut(n)] = g_rows.astype(BF16).reshape(EF, CAP, COLS)
            return 0

        lax.fori_loop(0, n_cols, step, 0)

    loads[0].wait()
    loads[1].wait()
    gather(0, s_own)

    source = (s_own, s_mir)

    def z_send(r, s):
        tz = lax.rem(z + DELTA[s], NZ)
        return remote(
            source[r].at[:, lax.div(tz, 2)], rows.at[:, r, s, 0], zs.at[r, s], zr.at[r, s], z_at(DELTA[s])
        )

    def y_send(r, s, way):
        return remote(
            rows.at[:, r, s, 0], rows.at[:, r, s, 1 + way], ys.at[way, r, s], yr.at[way, r, s], (y_up, y_dn)[way]
        )

    def forward(r, s, way):
        return remote(
            rows.at[way, r, s, 1 + way], rows.at[way, r, s, 3], fs.at[way, r, s], fr.at[way, r, s], (y_up, y_dn)[way]
        )

    cross = remote(s_out, s_mir, cs.at[0], cs.at[1], mirror)

    pl.semaphore_wait(barrier, len(partners))
    steps = [(r, s) for r in range(2) for s in range(NZ)]
    z_order = [(r, s) for r, s in steps if s > 0]
    issued = 0

    def issue_z(upto):
        nonlocal issued
        while issued < min(upto, len(z_order)):
            z_send(*z_order[issued]).start()
            issued += 1

    issue_z(4)
    rows[:, 0, 0, 0] = s_own[:, lax.div(z, 2)]
    for way in range(2):
        y_send(0, 0, way).start()

    loads[2].wait()
    loads[3].wait()
    gather(2, s_out)
    cross.start()

    for c in loads[4:]:
        c.wait()
    for n in range(n_cols):
        wgut[:, n * COLS : (n + 1) * COLS] = wgu[n * COLS : (n + 1) * COLS, :].T
        wdt[n * COLS : (n + 1) * COLS, :] = wd[:, n * COLS : (n + 1) * COLS].T

    def partial_send(c):
        r, k = c // 4, c % 4
        there = (1 - r) * 4 + k
        return remote(ps.at[c], pr.at[there], xs.at[c], xr.at[there], mirror)

    def partial_recv(c):
        return remote(ps.at[c], pr.at[c], xs.at[c], xr.at[c], mirror)

    def products(c):
        r, k = c // 4, c % 4
        gu = dot(rows[0, r, 2 * k : 2 * k + 2].reshape(128, half_width), wgu[...])
        dh = dot(rows[1, r, 2 * k : 2 * k + 2].reshape(128, half_width), wdt[...])
        pf[c, :, 0:256] = gu
        pf[c, :, 256:384] = dh
        ps[c, :, 0:256] = gu.astype(BF16)
        ps[c, :, 256:384] = dh.astype(BF16)
        partial_send(c).start()

    def activations(c):
        r, k = c // 4, c % 4
        partial_recv(c).wait_recv()
        full = pf[c] + pr[c].astype(F32)
        gate, up, dh = full[:, 0:128], full[:, 128:256], full[:, 256:384]
        sig = jax.nn.sigmoid(gate)
        act = gate * sig
        hidden = act * up
        d_gate = dh * up * sig * (1.0 + gate * (1.0 - sig))
        d_up = dh * act
        da[r, 2 * k : 2 * k + 2, :, :, 0:128] = d_gate.astype(BF16).reshape(2, NY, CAP, 128)
        da[r, 2 * k : 2 * k + 2, :, :, 128:256] = d_up.astype(BF16).reshape(2, NY, CAP, 128)
        span = slice(c * 128, (c + 1) * 128)
        dat[0:128, span] = d_gate.T.astype(BF16)
        dat[128:256, span] = d_up.T.astype(BF16)
        dat[256:384, span] = hidden.T.astype(BF16)

    def forward_step(i):
        r, s = steps[i]
        for way in range(2):
            y_send(r, s, way).wait_recv()
            forward(r, s, way).start()

    def finish_step(i):
        r, s = steps[i]
        for way in range(2):
            forward(r, s, way).wait_recv()

    def chunk_done(c):
        products(c)
        if c >= 4:
            activations(c)
        if c >= 5:
            activations(c - 5)

    for i, (r, s) in enumerate(steps):
        if i > 0:
            if s > 0:
                z_send(r, s).wait_recv()
            else:
                rows[:, r, 0, 0] = s_mir[:, lax.div(z, 2)]
            for way in range(2):
                y_send(r, s, way).start()
        if i == 3:
            cross.wait_recv()
        issue_z(i + 5)
        if i >= 1:
            forward_step(i - 1)
        if i >= 2:
            finish_step(i - 2)
            if (i - 2) % 2 == 1:
                chunk_done((i - 2) // 2)
    last = len(steps) - 1
    forward_step(last)
    finish_step(last - 1)
    finish_step(last)
    chunk_done(7)
    activations(3)

    def grad_copies(n):
        here = pl.ds(pl.multiple_of(col + n * COLS, 128), COLS)
        span = pl.ds(n * COLS, COLS)
        pairs = (
            (go_g.at[span, :], gg_h.at[here, :]),
            (go_u.at[span, :], ug_h.at[here, :]),
            (go_d.at[n], dg_h.at[:, here]),
        )
        for j, (src, dst) in enumerate(pairs):
            yield remote(src, dst, gs.at[n, j], gr.at[n, j], mirror), pltpu.make_async_copy(src, dst, gl.at[n, j])

    def grad_recv(n, j):
        there = pl.ds(pl.multiple_of(ocol + n * COLS, 128), COLS)
        span = pl.ds(n * COLS, COLS)
        src, dst = (
            (go_g.at[span, :], gg_h.at[there, :]),
            (go_u.at[span, :], ug_h.at[there, :]),
            (go_d.at[n], dg_h.at[:, there]),
        )[j]
        return remote(src, dst, gs.at[n, j], gr.at[n, j], mirror)

    def grads(n):
        span = slice(n * COLS, (n + 1) * COLS)
        gu = dot(dat[0:256, :], rows[0, :, :, :, :, span].reshape(1024, COLS)).T
        go_g[span, :] = gu[:, 0:128].astype(BF16)
        go_u[span, :] = gu[:, 128:256].astype(BF16)
        go_d[n] = dot(dat[256:384, :], rows[1, :, :, :, :, span].reshape(1024, COLS)).astype(BF16)
        for far, local in grad_copies(n):
            far.start()
            local.start()

    quarter = half_width // 2

    def anti_send(g, way):
        return remote(
            pb.at[:, pl.ds(2 * g, 2), 3, :, pl.ds(way * quarter, quarter)],
            anti.at[way, :, pl.ds(2 * g, 2)],
            ans.at[way, g],
            anr.at[way, g],
            (y_up, y_dn)[way],
        )

    def near_send(g, way):
        return remote(
            pb.at[:, pl.ds(2 * g, 2), 2 - way],
            near.at[way, :, pl.ds(2 * g, 2)],
            ns.at[way, g],
            nr.at[way, g],
            (y_up, y_dn)[way],
        )

    def parts(g):
        span = slice(2 * g, 2 * g + 2)
        lhs = da[:, span].reshape(256, 256)

        def step(n, _):
            part = dot(lhs, wgut[:, cut(n)])
            pb[:, span, :, :, cut(n)] = part.astype(BF16).reshape(2, 2, NY, CAP, COLS)
            return 0

        lax.fori_loop(0, n_cols, step, 0)
        for way in range(2):
            anti_send(g, way).start()

    def nears(g):
        span = slice(2 * g, 2 * g + 2)
        for way in range(2):
            anti_send(g, way).wait_recv()
            part = slice(way * quarter, (way + 1) * quarter)
            total = pb[:, span, 2 - way, :, part].astype(F32) + anti[way, :, span].astype(F32)
            pb[:, span, 2 - way, :, part] = total.astype(BF16)
            near_send(g, way).start()

    def home_send(s):
        back = NZ - DELTA[s]
        return remote(fin.at[s], home.at[z], hs.at[s], hr.at[s], z_at(back))

    def home_recv(s):
        return remote(fin.at[s], home.at[lax.rem(z + DELTA[s], NZ)], hs.at[s], hr.at[s], z_at(NZ - DELTA[s]))

    def sums(g):
        span = slice(2 * g, 2 * g + 2)
        for way in range(2):
            near_send(g, way).wait_recv()
        for s in range(2 * g, 2 * g + 2):
            total = pb[:, s, 0].astype(F32) + near[0, :, s].astype(F32) + near[1, :, s].astype(F32)
            if s == 0:
                home[z] = total.astype(BF16)
            else:
                fin[s] = total.astype(BF16)
                home_send(s).start()

    parts(3)
    grads(0)
    parts(2)
    nears(3)
    grads(1)
    parts(1)
    nears(2)
    grads(2)
    parts(0)
    nears(1)
    grads(3)
    sums(3)
    nears(0)
    grads(4)
    sums(2)
    grads(5)
    sums(1)
    grads(6)
    sums(0)

    for s in range(1, NZ):
        home_recv(s).wait_recv()
    for e in range(EF):
        both = home[2 * e].astype(F32) + home[2 * e + 1].astype(F32)
        slots[e * CAP : (e + 1) * CAP, :] = both[0].astype(BF16)
        slots_m[e * CAP : (e + 1) * CAP, :] = both[1].astype(BF16)
    swap = remote(slots_m, slots_o, cs.at[2], cs.at[3], mirror)
    swap.start()

    def place(index, value):
        def step(n, _):
            got = dot(pmat_t[:, 0 : EF * CAP], value[:, cut(n)])
            out[index, :, cut(n)] = got.astype(BF16)
            return 0

        lax.fori_loop(0, n_cols, step, 0)

    place(0, slots)
    first = pltpu.make_async_copy(out.at[0], ig_h.at[:, pl.ds(col, half_width)], ol.at[0])
    first.start()
    swap.wait_recv()
    place(1, slots_o)
    second = pltpu.make_async_copy(out.at[1], ig_h.at[:, pl.ds(ocol, half_width)], ol.at[1])
    second.start()

    for n in range(n_cols):
        for j in range(3):
            grad_recv(n, j).wait_recv()
        for far, local in grad_copies(n):
            far.wait_send()
            local.wait()
    for r, s in steps:
        if s > 0:
            z_send(r, s).wait_send()
        for way in range(2):
            y_send(r, s, way).wait_send()
            forward(r, s, way).wait_send()
    for c in range(8):
        partial_send(c).wait_send()
    for g in range(4):
        for way in range(2):
            anti_send(g, way).wait_send()
            near_send(g, way).wait_send()
    for s in range(1, NZ):
        home_send(s).wait_send()
    cross.wait_send()
    swap.wait_send()
    first.wait()
    second.wait()


def body(layer_input, out_grad, combine_weights, expert_ids, w_gate, w_up, w_down):
    tokens, width = layer_input.shape[1:]
    h = width // 2
    n_cols = h // COLS
    dma = pltpu.SemaphoreType.DMA
    outs = pl.pallas_call(
        kernel,
        out_shape=(
            jax.ShapeDtypeStruct((tokens, width), BF16),
            jax.ShapeDtypeStruct((width, 128), BF16),
            jax.ShapeDtypeStruct((width, 128), BF16),
            jax.ShapeDtypeStruct((128, width), BF16),
        ),
        in_specs=[VMEM, VMEM, ANY, ANY, ANY, ANY, ANY],
        out_specs=(ANY, ANY, ANY, ANY),
        scratch_shapes=[
            pltpu.VMEM((4, tokens, h), BF16),
            pltpu.VMEM((h, 256), BF16),
            pltpu.VMEM((128, h), BF16),
            pltpu.VMEM((256, h), BF16),
            pltpu.VMEM((h, 128), BF16),
            pltpu.VMEM((128, tokens), BF16),
            pltpu.VMEM((tokens, 128), BF16),
            pltpu.VMEM((128, 1), F32),
            pltpu.VMEM((2, EF, CAP, h), BF16),
            pltpu.VMEM((2, EF, CAP, h), BF16),
            pltpu.VMEM((2, EF, CAP, h), BF16),
            pltpu.VMEM((2, 2, NZ, NY, CAP, h), BF16),
            pltpu.VMEM((8, 128, 384), F32),
            pltpu.VMEM((8, 128, 384), BF16),
            pltpu.VMEM((8, 128, 384), BF16),
            pltpu.VMEM((2, NZ, NY, CAP, 256), BF16),
            pltpu.VMEM((384, 1024), BF16),
            pltpu.VMEM((h, 128), BF16),
            pltpu.VMEM((h, 128), BF16),
            pltpu.VMEM((n_cols, 128, COLS), BF16),
            pltpu.VMEM((2, NZ, NY, CAP, h), BF16),
            pltpu.VMEM((2, 2, NZ, CAP, h // 2), BF16),
            pltpu.VMEM((2, 2, NZ, CAP, h), BF16),
            pltpu.VMEM((NZ, 2, CAP, h), BF16),
            pltpu.VMEM((NZ, 2, CAP, h), BF16),
            pltpu.VMEM((EF * CAP, h), BF16),
            pltpu.VMEM((EF * CAP, h), BF16),
            pltpu.VMEM((EF * CAP, h), BF16),
            pltpu.VMEM((2, tokens, h), BF16),
            dma((7,)),
            dma((1,)),
            dma((2, NZ)),
            dma((2, NZ)),
            dma((2, 2, NZ)),
            dma((2, 2, NZ)),
            dma((2, 2, NZ)),
            dma((2, 2, NZ)),
            dma((8,)),
            dma((8,)),
            dma((4,)),
            dma((2, 4)),
            dma((2, 4)),
            dma((2, 4)),
            dma((2, 4)),
            dma((NZ,)),
            dma((NZ,)),
            dma((n_cols, 3)),
            dma((n_cols, 3)),
            dma((n_cols, 3)),
            dma((2,)),
        ],
        compiler_params=pltpu.CompilerParams(
            collective_id=0, has_side_effects=True, vmem_limit_bytes=56 * 1024 * 1024
        ),
    )(
        expert_ids[0],
        combine_weights[0],
        layer_input[0],
        out_grad[0],
        w_gate[0],
        w_up[0],
        w_down[0],
    )
    return tuple(o[None] for o in outs)


def solution(mesh):
    return jax.shard_map(
        body,
        mesh=mesh,
        in_specs=(
            P("pipe", "expert", None),
            P("pipe", "expert", None),
            P("pipe", "expert", None),
            P("pipe", "expert", None),
            P("pipe", None, "expert"),
            P("pipe", None, "expert"),
            P("pipe", "expert", None),
        ),
        out_specs=(
            P("pipe", "expert", None),
            P("pipe", None, "expert"),
            P("pipe", None, "expert"),
            P("pipe", "expert", None),
        ),
        check_vma=False,
    )
```

time: 365 us -> 141 us (0.39)
  waiting for transfers between devices: 273 us -> 0 us
  Pallas kernels: 0 us -> 131 us
  starting transfers between devices: 45.6 us -> 0 us
  matrix products: 24 us -> 0 us
  other arithmetic: 15.5 us -> 0 us
    all_to_all x4 -> x0, waiting for transfers between devices: 163 us -> none  [the longest x1 80 us: body(): lax.all_to_all(copies_input, 'expert', split_axis=0, concat_axis=0, tiled...]
    pallas_call x0 -> x1, Pallas kernels: none -> 131 us  [body(): pl.pallas_call(kernel, out_shape=(jax.ShapeDtypeStruct((tokens, width), B...]
    ppermute x9 -> x0, waiting for transfers between devices: 109 us -> none  [partner_2(): lax.ppermute(shard, axis, [(i, i ^ 1 << bit) for i in range(lax.axis_size...]
    all_to_all x4 -> x0, starting transfers between devices: 31 us -> none  [the longest x1 12 us: body(): lax.all_to_all(copies_scale.astype(jnp.bfloat16), 'expert', split_axis=0,...]
    dot_general x11 -> x0, matrix products: 24 us -> none  [the longest x1 3.22 us: body(): jnp.dot(rows_input, gate_local, preferred_element_type=jnp.float32)]
    ppermute x9 -> x0, starting transfers between devices: 14.6 us -> none  [partner_2(): lax.ppermute(shard, axis, [(i, i ^ 1 << bit) for i in range(lax.axis_size...]
    unnamed x10 -> x12, local copies, waits for them, and re-layouts: 0.08 us -> 8.73 us
    convert_element_type x5 -> x0, other arithmetic: 6.37 us -> none  [the longest x2 6.3 us: body(): (got_scale.reshape(slot_rows, 1) * rows_grad.astype(jnp.float32)).astype(...]
  transfers between devices with their start and end apart: 13 -> 0, of which waited for: 10 -> 0; matrix products, arithmetic and copies ran while one was open for 6% -> 0% of each run, Pallas kernels for 0% -> 0%
where the time goes in v1:
time: 141 us
  Pallas kernels  131 us (93%)
  local copies, waits for them, and re-layouts  8.73 us (6%)
    pallas_call x1, Pallas kernels, body(): pl.pallas_call(kernel, out_shape=(jax.ShapeDtypeStruct((tokens, width), B...  131 us
    unnamed x12, local copies, waits for them, and re-layouts  8.73 us

profile of v1, /device:TPU:1, one launch (start us, length us, event | category | flops | bytes accessed | tf_op | source)
XLA Modules:
  0.0 140.6 jit_solution(9753374783828062152)
XLA Ops:
  0.6 1.5 %copy.12 = f32[1,256,8]{2,1,0:T(8,128)} copy(f32[1,256,8]{1,2,0:T(8,128)} %param.9) | data formatting | bytes 16384 | tf_op args[2]
  2.1 1.5 %copy.11 = s32[1,256,8]{2,1,0:T(8,128)} copy(s32[1,256,8]{1,2,0:T(8,128)} %param.10) | data formatting | bytes 16384 | tf_op args[3]
  3.6 131.2 %shard_map.102 = (bf16[256,3584]{1,0:T(8,128)(2,1)}, bf16[3584,128]{1,0:T(8,128)(2,1)}, bf16[3584,128]{1,0:T(8,128)(2,1)}, bf16[128,3584]{1,0:T(8,128)(2,1)}) custom-call(s32[256,8]{1,0:T(8,128)} %bitcast.21, f32[256,8]{1,0:T(8,128)} %bitcast.20, bf16[256,3584]{1,0:T(8,128)(2,1)} %bitcast.12, bf16[256,3584]{1,0:T(8,128)(2,1)} %bitcast.13, ...), custom_call_target="tpu_custom_call" | custom-call | tf_op jit(solution)/shard_map/pallas_call | solution.py:455
  134.8 0.0 copy-start.2
  134.8 0.0 copy-start.1
  134.8 3.0 %copy.17 = bf16[1,256,3584]{2,1,0:T(8,128)(2,1)} copy(bf16[1,256,3584]{2,1,0:T(8,128)(2,1)} %bitcast.11) | data formatting | bytes 3670016
  137.8 0.0 copy-done.2
  137.8 0.0 copy-start
  137.8 0.9 copy.18
  138.7 0.0 copy-done.1
  138.7 0.9 copy.19
  139.6 0.0 copy-done
  139.6 0.9 copy.20
Async XLA Ops:
  134.8 3.0 %copy-start.2 = (bf16[3584,128]{1,0:T(8,128)(2,1)S(1)}, bf16[3584,128]{1,0:T(8,128)(2,1)}, u32[]{:S(2)}) copy-start(bf16[3584,128]{1,0:T(8,128)(2,1)} %get-tuple-element.9) | copy-start | bytes 2752516
  134.8 3.9 %copy-start.1 = (bf16[3584,128]{1,0:T(8,128)(2,1)S(1)}, bf16[3584,128]{1,0:T(8,128)(2,1)}, u32[]{:S(2)}) copy-start(bf16[3584,128]{1,0:T(8,128)(2,1)} %get-tuple-element.10) | copy-start | bytes 2752516
  137.8 1.9 %copy-start = (bf16[128,3584]{1,0:T(8,128)(2,1)S(1)}, bf16[128,3584]{1,0:T(8,128)(2,1)}, u32[]{:S(2)}) copy-start(bf16[128,3584]{1,0:T(8,128)(2,1)} %get-tuple-element.11) | copy-start | bytes 2752516

commit v2 on v1

--- a/solution.py
+++ b/solution.py
@@ -12,8 +12,12 @@
 NY = 4
 NZ = 8
 EF = 4
+AHEAD = 3
+CROSS_AT = 5
+HANDED = ((0, 0), (0, 1), (0, 2), (0, 3), (1, 1), (1, 2))
+RELAYED = ((0, 2), (0, 3), (1, 2), (1, 3))
+ORDER = ((0, 2, 1, 4, 3, 6, 5, 7), (2, 4, 3, 6, 5, 0, 7, 1))
 CAP = 16
-DELTA = (0, 1, 7, 2, 6, 3, 5, 4)
 COLS = 256
 ANY = pl.BlockSpec(memory_space=pl.ANY)
 VMEM = pl.BlockSpec(memory_space=pltpu.VMEM)
@@ -31,7 +35,8 @@
     wg_h,
     wu_h,
     wd_h,
-    ig_h,
+    so_h,
+    pm_h,
     gg_h,
     ug_h,
     dg_h,
@@ -62,12 +67,13 @@
     home,
     slots,
     slots_m,
-    slots_o,
-    out,
     lsem,
-    bsem,
     zs,
     zr,
+    c0s,
+    c0r,
+    c3s,
+    c3r,
     ys,
     yr,
     fs,
@@ -75,6 +81,8 @@
     xs,
     xr,
     cs,
+    ss,
+    sr,
     ans,
     anr,
     ns,
@@ -100,8 +108,17 @@
     y_up = (p, z * NY + lax.rem(y + 1, NY))
     y_dn = (p, z * NY + lax.rem(y + NY - 1, NY))
 
+    odd = lax.rem(z, 2)
+    sign = 2 * odd - 1
+
     def z_at(delta):
-        return (p, lax.rem(z + delta, NZ) * NY + y)
+        return (p, lax.rem(z + delta + NZ, NZ) * NY + y)
+
+    pair = z_at(-sign)
+
+    def toward(s):
+        delta = (1 - 2 * lax.rem(z + s // 2, 2)) * (s // 2 + s % 2)
+        return delta, lax.div(lax.rem(z + delta + NZ, NZ), 2)
 
     def remote(src, dst, send, recv, device):
         return pltpu.make_async_remote_copy(
@@ -128,23 +145,25 @@
     for device in partners:
         pl.semaphore_signal(barrier, inc=1, device_id=device, device_id_type=MESH)
 
-    lane = lax.broadcasted_iota(jnp.int32, (tokens, 128), 1)
-    lane_expert = lax.div(lane, CAP)
-    named = jnp.zeros((tokens, 128), F32)
-    weight = jnp.zeros((tokens, 128), F32)
-    for k in range(ids.shape[1]):
-        hit = ids[:, k : k + 1] == lane_expert
+    row = lax.broadcasted_iota(jnp.int32, (128, tokens), 0)
+    row_expert = lax.div(row, CAP)
+    named = jnp.zeros((128, tokens), F32)
+    weight = jnp.zeros((128, tokens), F32)
+    for k in range(ids.shape[0]):
+        hit = ids[k : k + 1, :] == row_expert
         named = jnp.where(hit, 1.0, named)
-        weight = jnp.where(hit, probs[:, k : k + 1], weight)
-    named = jnp.where(lane < EF * CAP, named, 0.0)
+        weight = jnp.where(hit, probs[k : k + 1, :], weight)
+    named = jnp.where(row < EF * CAP, named, 0.0)
     before = (
-        lax.broadcasted_iota(jnp.int32, (tokens, tokens), 0) > lax.broadcasted_iota(jnp.int32, (tokens, tokens), 1)
+        lax.broadcasted_iota(jnp.int32, (tokens, tokens), 0) < lax.broadcasted_iota(jnp.int32, (tokens, tokens), 1)
     ).astype(F32)
-    count = dot(before.astype(BF16), named.astype(BF16))
-    placed = jnp.where(count == lax.rem(lane, CAP).astype(F32), named, 0.0)
-    pmat_t[...] = placed.astype(BF16)
-    pmat[...] = placed.T.astype(BF16)
-    wslot[...] = jnp.sum((placed * weight).T, axis=1, keepdims=True)
+    count = dot(named.astype(BF16), before.astype(BF16))
+    placed = jnp.where(count == lax.rem(row, CAP).astype(F32), named, 0.0)
+    pmat[...] = placed.astype(BF16)
+    pmat_t[...] = placed.T.astype(BF16)
+    wslot[...] = jnp.sum(placed * weight, axis=1, keepdims=True)
+    save = pltpu.make_async_copy(pmat_t, pm_h, ol.at[0])
+    save.start()
 
     def gather(base, dst):
         def step(n, _):
@@ -163,10 +182,11 @@
     source = (s_own, s_mir)
 
     def z_send(r, s):
-        tz = lax.rem(z + DELTA[s], NZ)
-        return remote(
-            source[r].at[:, lax.div(tz, 2)], rows.at[:, r, s, 0], zs.at[r, s], zr.at[r, s], z_at(DELTA[s])
-        )
+        delta, expert = toward(s)
+        return remote(source[r].at[:, expert], rows.at[:, r, s, 0], zs.at[r, s], zr.at[r, s], z_at(delta))
+
+    def relay(r, j):
+        return remote(rows.at[:, r, 2 * j, 0], rows.at[:, r, 2 * j + 1, 0], c0s.at[r, j], c0r.at[r, j], pair)
 
     def y_send(r, s, way):
         return remote(
@@ -178,23 +198,46 @@
             rows.at[way, r, s, 1 + way], rows.at[way, r, s, 3], fs.at[way, r, s], fr.at[way, r, s], (y_up, y_dn)[way]
         )
 
+    def hand(r, j, way):
+        return remote(
+            rows.at[way, r, 2 * j, 3], rows.at[way, r, 2 * j + 1, 3], c3s.at[way, r, j], c3r.at[way, r, j], pair
+        )
+
+    def handed(r, s):
+        return s % 2 == 1 and (r, s // 2) in HANDED
+
     cross = remote(s_out, s_mir, cs.at[0], cs.at[1], mirror)
 
     pl.semaphore_wait(barrier, len(partners))
-    steps = [(r, s) for r in range(2) for s in range(NZ)]
-    z_order = [(r, s) for r, s in steps if s > 0]
+    steps = [(r, s) for r in range(2) for s in ORDER[r]]
+    ready = [s // 2 for s in ORDER[1] if s % 2]
+    z_order = [(i, r, s) for i, (r, s) in enumerate(steps) if s > 0 and not (s % 2 and (r, s // 2) in RELAYED)]
     issued = 0
 
-    def issue_z(upto):
+    def issue_z(now):
         nonlocal issued
-        while issued < min(upto, len(z_order)):
-            z_send(*z_order[issued]).start()
+        while issued < len(z_order):
+            i, r, s = z_order[issued]
+            if i > now + AHEAD or (r == 1 and now < CROSS_AT):
+                break
+            z_send(r, s).start()
             issued += 1
 
-    issue_z(4)
-    rows[:, 0, 0, 0] = s_own[:, lax.div(z, 2)]
-    for way in range(2):
-        y_send(0, 0, way).start()
+    def arrive(i):
+        r, s = steps[i]
+        if s == 0:
+            rows[:, r, 0, 0] = source[r][:, lax.div(z, 2)]
+        elif s % 2 and (r, s // 2) in RELAYED:
+            relay(r, s // 2).wait_recv()
+        else:
+            z_send(r, s).wait_recv()
+        if s % 2 == 0 and (r, s // 2) in RELAYED:
+            relay(r, s // 2).start()
+        for way in range(2):
+            y_send(r, s, way).start()
+
+    issue_z(0)
+    arrive(0)
 
     loads[2].wait()
     loads[3].wait()
@@ -246,43 +289,28 @@
         r, s = steps[i]
         for way in range(2):
             y_send(r, s, way).wait_recv()
-            forward(r, s, way).start()
-
-    def finish_step(i):
+            if not handed(r, s):
+                forward(r, s, way).start()
+
+    def hand_step(i):
         r, s = steps[i]
-        for way in range(2):
-            forward(r, s, way).wait_recv()
-
-    def chunk_done(c):
-        products(c)
-        if c >= 4:
-            activations(c)
-        if c >= 5:
-            activations(c - 5)
-
-    for i, (r, s) in enumerate(steps):
-        if i > 0:
-            if s > 0:
-                z_send(r, s).wait_recv()
+        if s % 2 == 0 and (r, s // 2) in HANDED:
+            for way in range(2):
+                forward(r, s, way).wait_recv()
+                hand(r, s // 2, way).start()
+
+    def chunk_done(r, j):
+        for way in range(2):
+            if (r, j) in HANDED:
+                hand(r, j, way).wait_recv()
             else:
-                rows[:, r, 0, 0] = s_mir[:, lax.div(z, 2)]
-            for way in range(2):
-                y_send(r, s, way).start()
-        if i == 3:
-            cross.wait_recv()
-        issue_z(i + 5)
-        if i >= 1:
-            forward_step(i - 1)
-        if i >= 2:
-            finish_step(i - 2)
-            if (i - 2) % 2 == 1:
-                chunk_done((i - 2) // 2)
-    last = len(steps) - 1
-    forward_step(last)
-    finish_step(last - 1)
-    finish_step(last)
-    chunk_done(7)
-    activations(3)
+                forward(r, 2 * j, way).wait_recv()
+                forward(r, 2 * j + 1, way).wait_recv()
+        products(r * 4 + j)
+        if r == 1:
+            activations(4 + j)
+            if j != ready[0]:
+                activations(ready[ready.index(j) - 1])
 
     def grad_copies(n):
         here = pl.ds(pl.multiple_of(col + n * COLS, 128), COLS)
@@ -358,11 +386,9 @@
             near_send(g, way).start()
 
     def home_send(s):
-        back = NZ - DELTA[s]
-        return remote(fin.at[s], home.at[z], hs.at[s], hr.at[s], z_at(back))
-
-    def home_recv(s):
-        return remote(fin.at[s], home.at[lax.rem(z + DELTA[s], NZ)], hs.at[s], hr.at[s], z_at(NZ - DELTA[s]))
+        j = s // 2
+        back = sign * j if s % 2 == 0 else -sign * (1 + j)
+        return remote(fin.at[s], home.at[s], hs.at[s], hr.at[s], z_at(back))
 
     def sums(g):
         span = slice(2 * g, 2 * g + 2)
@@ -371,55 +397,80 @@
         for s in range(2 * g, 2 * g + 2):
             total = pb[:, s, 0].astype(F32) + near[0, :, s].astype(F32) + near[1, :, s].astype(F32)
             if s == 0:
-                home[z] = total.astype(BF16)
+                home[0] = total.astype(BF16)
             else:
                 fin[s] = total.astype(BF16)
                 home_send(s).start()
 
-    parts(3)
+    def slot_copies(j):
+        _, expert = toward(2 * j)
+        dst = so_h.at[expert, :, pl.ds(col, half_width)]
+        return (
+            pltpu.make_async_copy(slots.at[j], dst, ol.at[1 + j]),
+            remote(slots_m.at[j], dst, ss.at[j], sr.at[j], mirror),
+        )
+
+    def slot_recv(j):
+        _, expert = toward(2 * j)
+        return remote(slots_m.at[j], so_h.at[expert, :, pl.ds(ocol, half_width)], ss.at[j], sr.at[j], mirror)
+
+    def gather_home(j):
+        for s in (2 * j, 2 * j + 1):
+            if s > 0:
+                home_send(s).wait_recv()
+        both = home[2 * j].astype(F32) + home[2 * j + 1].astype(F32)
+        slots_m[j] = both[1].astype(BF16)
+        local, far = slot_copies(j)
+        far.start()
+        slots[j] = both[0].astype(BF16)
+        local.start()
+
+    pending = []
+    for i in range(len(steps)):
+        r, s = steps[i]
+        if i > 0:
+            arrive(i)
+        if i == CROSS_AT:
+            cross.wait_recv()
+        issue_z(i)
+        if i >= 1:
+            forward_step(i - 1)
+        if i >= 2:
+            hand_step(i - 2)
+        if s % 2 == 1:
+            pending.append((i + (3 if (r, s // 2) in HANDED else 2), r, s // 2))
+        while pending and pending[0][0] <= i:
+            _, r, j = pending.pop(0)
+            chunk_done(r, j)
+    forward_step(15)
+    hand_step(14)
+    parts(ready[0])
+    while len(pending) > 1:
+        chunk_done(*pending.pop(0)[1:])
+    parts(ready[1])
+    chunk_done(*pending.pop(0)[1:])
+    nears(ready[0])
+    activations(ready[3])
     grads(0)
-    parts(2)
-    nears(3)
+    parts(ready[2])
+    nears(ready[1])
     grads(1)
-    parts(1)
-    nears(2)
+    sums(ready[0])
+    parts(ready[3])
+    nears(ready[2])
     grads(2)
-    parts(0)
-    nears(1)
+    sums(ready[1])
+    gather_home(ready[0])
+    nears(ready[3])
     grads(3)
-    sums(3)
-    nears(0)
     grads(4)
-    sums(2)
+    sums(ready[2])
+    gather_home(ready[1])
     grads(5)
-    sums(1)
     grads(6)
-    sums(0)
-
-    for s in range(1, NZ):
-        home_recv(s).wait_recv()
-    for e in range(EF):
-        both = home[2 * e].astype(F32) + home[2 * e + 1].astype(F32)
-        slots[e * CAP : (e + 1) * CAP, :] = both[0].astype(BF16)
-        slots_m[e * CAP : (e + 1) * CAP, :] = both[1].astype(BF16)
-    swap = remote(slots_m, slots_o, cs.at[2], cs.at[3], mirror)
-    swap.start()
-
-    def place(index, value):
-        def step(n, _):
-            got = dot(pmat_t[:, 0 : EF * CAP], value[:, cut(n)])
-            out[index, :, cut(n)] = got.astype(BF16)
-            return 0
-
-        lax.fori_loop(0, n_cols, step, 0)
-
-    place(0, slots)
-    first = pltpu.make_async_copy(out.at[0], ig_h.at[:, pl.ds(col, half_width)], ol.at[0])
-    first.start()
-    swap.wait_recv()
-    place(1, slots_o)
-    second = pltpu.make_async_copy(out.at[1], ig_h.at[:, pl.ds(ocol, half_width)], ol.at[1])
-    second.start()
+    sums(ready[3])
+    gather_home(ready[2])
+    gather_home(ready[3])
 
     for n in range(n_cols):
         for j in range(3):
@@ -428,11 +479,16 @@
             far.wait_send()
             local.wait()
     for r, s in steps:
-        if s > 0:
+        if s % 2 and (r, s // 2) in RELAYED:
+            relay(r, s // 2).wait_send()
+        elif s > 0:
             z_send(r, s).wait_send()
         for way in range(2):
             y_send(r, s, way).wait_send()
-            forward(r, s, way).wait_send()
+            if not handed(r, s):
+                forward(r, s, way).wait_send()
+            if s % 2 == 0 and (r, s // 2) in HANDED:
+                hand(r, s // 2, way).wait_send()
     for c in range(8):
         partial_send(c).wait_send()
     for g in range(4):
@@ -442,9 +498,19 @@
     for s in range(1, NZ):
         home_send(s).wait_send()
     cross.wait_send()
-    swap.wait_send()
-    first.wait()
-    second.wait()
+    save.wait()
+    for j in range(4):
+        local, far = slot_copies(j)
+        far.wait_send()
+        local.wait()
+        slot_recv(j).wait_recv()
+
+
+def finish(slots, pmat_t, gate, up, down, ig, gate_o, up_o, down_o):
+    ig[...] = dot(pmat_t[:, 0 : EF * CAP], slots[...]).astype(BF16)
+    gate_o[...] = gate[...]
+    up_o[...] = up[...]
+    down_o[...] = down[...]
 
 
 def body(layer_input, out_grad, combine_weights, expert_ids, w_gate, w_up, w_down):
@@ -455,13 +521,14 @@
     outs = pl.pallas_call(
         kernel,
         out_shape=(
-            jax.ShapeDtypeStruct((tokens, width), BF16),
+            jax.ShapeDtypeStruct((EF, CAP, width), BF16),
+            jax.ShapeDtypeStruct((tokens, 128), BF16),
             jax.ShapeDtypeStruct((width, 128), BF16),
             jax.ShapeDtypeStruct((width, 128), BF16),
             jax.ShapeDtypeStruct((128, width), BF16),
         ),
         in_specs=[VMEM, VMEM, ANY, ANY, ANY, ANY, ANY],
-        out_specs=(ANY, ANY, ANY, ANY),
+        out_specs=(ANY, ANY, ANY, ANY, ANY),
         scratch_shapes=[
             pltpu.VMEM((4, tokens, h), BF16),
             pltpu.VMEM((h, 256), BF16),
@@ -488,20 +555,23 @@
             pltpu.VMEM((2, 2, NZ, CAP, h), BF16),
             pltpu.VMEM((NZ, 2, CAP, h), BF16),
             pltpu.VMEM((NZ, 2, CAP, h), BF16),
-            pltpu.VMEM((EF * CAP, h), BF16),
-            pltpu.VMEM((EF * CAP, h), BF16),
-            pltpu.VMEM((EF * CAP, h), BF16),
-            pltpu.VMEM((2, tokens, h), BF16),
+            pltpu.VMEM((EF, CAP, h), BF16),
+            pltpu.VMEM((EF, CAP, h), BF16),
             dma((7,)),
-            dma((1,)),
             dma((2, NZ)),
             dma((2, NZ)),
+            dma((2, 4)),
+            dma((2, 4)),
+            dma((2, 2, 4)),
+            dma((2, 2, 4)),
             dma((2, 2, NZ)),
             dma((2, 2, NZ)),
             dma((2, 2, NZ)),
             dma((2, 2, NZ)),
             dma((8,)),
             dma((8,)),
+            dma((2,)),
+            dma((4,)),
             dma((4,)),
             dma((2, 4)),
             dma((2, 4)),
@@ -512,21 +582,46 @@
             dma((n_cols, 3)),
             dma((n_cols, 3)),
             dma((n_cols, 3)),
-            dma((2,)),
+            dma((5,)),
         ],
         compiler_params=pltpu.CompilerParams(
             collective_id=0, has_side_effects=True, vmem_limit_bytes=56 * 1024 * 1024
         ),
     )(
-        expert_ids[0],
-        combine_weights[0],
+        expert_ids[0].T,
+        combine_weights[0].T,
         layer_input[0],
         out_grad[0],
         w_gate[0],
         w_up[0],
         w_down[0],
     )
-    return tuple(o[None] for o in outs)
+    slots, pmat_t, gate, up, down = outs
+    block = width // 2
+    results = pl.pallas_call(
+        finish,
+        grid=(width // block,),
+        out_shape=(
+            jax.ShapeDtypeStruct((tokens, width), BF16),
+            jax.ShapeDtypeStruct((width, 128), BF16),
+            jax.ShapeDtypeStruct((width, 128), BF16),
+            jax.ShapeDtypeStruct((128, width), BF16),
+        ),
+        in_specs=[
+            pl.BlockSpec((EF * CAP, block), lambda i: (0, i)),
+            pl.BlockSpec((tokens, 128), lambda i: (0, 0)),
+            pl.BlockSpec((block, 128), lambda i: (i, 0)),
+            pl.BlockSpec((block, 128), lambda i: (i, 0)),
+            pl.BlockSpec((128, block), lambda i: (0, i)),
+        ],
+        out_specs=(
+            pl.BlockSpec((tokens, block), lambda i: (0, i)),
+            pl.BlockSpec((block, 128), lambda i: (i, 0)),
+            pl.BlockSpec((block, 128), lambda i: (i, 0)),
+            pl.BlockSpec((128, block), lambda i: (0, i)),
+        ),
+    )(slots.reshape(EF * CAP, width), pmat_t, gate, up, down)
+    return tuple(o[None] for o in results)
 
 
 def solution(mesh):

time: 141 us -> 123 us (0.87)
  Pallas kernels: 131 us -> 122 us
  local copies, waits for them, and re-layouts: 8.73 us -> 0 us
    pallas_call x1 -> x2, Pallas kernels: 131 us -> 122 us  [the longest x1 118 us: body(): pl.pallas_call(kernel, out_shape=(jax.ShapeDtypeStruct((EF, CAP, width),...]
    unnamed x12 -> x0, local copies, waits for them, and re-layouts: 8.73 us -> none
where the time goes in v2:
time: 123 us
  Pallas kernels  122 us (99%)
    pallas_call x1, Pallas kernels, body(): pl.pallas_call(kernel, out_shape=(jax.ShapeDtypeStruct((EF, CAP, width),...  118 us
    pallas_call x1, Pallas kernels, body(): pl.pallas_call(finish, grid=(width // block,), out_shape=(jax.ShapeDtypeS...  4.06 us

profile of v2, /device:TPU:1, one launch (start us, length us, event | category | flops | bytes accessed | tf_op | source)
XLA Modules:
  0.0 122.8 jit_solution(3243100902128216175)
XLA Ops:
  0.6 118.1 %shard_map.102 = (bf16[4,16,3584]{2,1,0:T(8,128)(2,1)}, bf16[256,128]{1,0:T(8,128)(2,1)}, bf16[3584,128]{1,0:T(8,128)(2,1)}, bf16[3584,128]{1,0:T(8,128)(2,1)}, bf16[128,3584]{1,0:T(8,128)(2,1)}) custom-call(s32[8,256]{1,0:T(8,128)} %bitcast.22, f32[8,256]{1,0:T(8,128)} %bitcast.23, bf16[256,3584]{1,0:T(8,128)(2,1)} %bitcast.16, bf16[256,3584]{1,0:T(8,128)(2,1)} %bitcast.17, ...), custom_call_target="tpu_custom_call" | custom-call | tf_op jit(solution)/shard_map/pallas_call | solution.py:521
  118.7 4.1 %shard_map.103 = (bf16[256,3584]{1,0:T(8,128)(2,1)}, bf16[3584,128]{1,0:T(8,128)(2,1)}, bf16[3584,128]{1,0:T(8,128)(2,1)}, bf16[128,3584]{1,0:T(8,128)(2,1)}) custom-call(bf16[64,3584]{1,0:T(8,128)(2,1)} %bitcast.21, bf16[256,128]{1,0:T(8,128)(2,1)} %get-tuple-element.14.pmat_t, bf16[3584,128]{1,0:T(8,128)(2,1)} %get-tuple-element.15.gate, ...), custom_call_target="tpu_custom_call" | custom-call | tf_op jit(solution)/shard_map/pallas_call | solution.py:601

commit v3 on v2

--- a/solution.py
+++ b/solution.py
@@ -13,7 +13,8 @@
 NZ = 8
 EF = 4
 AHEAD = 3
-CROSS_AT = 5
+CROSS_AT = 6
+LAG = 3
 HANDED = ((0, 0), (0, 1), (0, 2), (0, 3), (1, 1), (1, 2))
 RELAYED = ((0, 2), (0, 3), (1, 2), (1, 3))
 ORDER = ((0, 2, 1, 4, 3, 6, 5, 7), (2, 4, 3, 6, 5, 0, 7, 1))
@@ -250,27 +251,33 @@
         wgut[:, n * COLS : (n + 1) * COLS] = wgu[n * COLS : (n + 1) * COLS, :].T
         wdt[n * COLS : (n + 1) * COLS, :] = wd[:, n * COLS : (n + 1) * COLS].T
 
-    def partial_send(c):
+    def partial_copy(c, there, first, count):
+        span = pl.ds(first, count)
+        k = first // 64
+        return remote(ps.at[c, span], pr.at[there, span], xs.at[c, k], xr.at[there, k], mirror)
+
+    def spans(c):
+        return ((0, 64), (64, 64)) if c % 4 == ready[3] and c >= 4 else ((0, 128),)
+
+    def partial_send(c, first, count):
+        return partial_copy(c, (c + 4) % 8, first, count)
+
+    def products(c, first=0, count=128):
         r, k = c // 4, c % 4
-        there = (1 - r) * 4 + k
-        return remote(ps.at[c], pr.at[there], xs.at[c], xr.at[there], mirror)
-
-    def partial_recv(c):
-        return remote(ps.at[c], pr.at[c], xs.at[c], xr.at[c], mirror)
-
-    def products(c):
-        r, k = c // 4, c % 4
-        gu = dot(rows[0, r, 2 * k : 2 * k + 2].reshape(128, half_width), wgu[...])
-        dh = dot(rows[1, r, 2 * k : 2 * k + 2].reshape(128, half_width), wdt[...])
-        pf[c, :, 0:256] = gu
-        pf[c, :, 256:384] = dh
-        ps[c, :, 0:256] = gu.astype(BF16)
-        ps[c, :, 256:384] = dh.astype(BF16)
-        partial_send(c).start()
+        slot = slice(2 * k + first // 64, 2 * k + (first + count) // 64)
+        gu = dot(rows[0, r, slot].reshape(count, half_width), wgu[...])
+        dh = dot(rows[1, r, slot].reshape(count, half_width), wdt[...])
+        span = slice(first, first + count)
+        pf[c, span, 0:256] = gu
+        pf[c, span, 256:384] = dh
+        ps[c, span, 0:256] = gu.astype(BF16)
+        ps[c, span, 256:384] = dh.astype(BF16)
+        partial_send(c, first, count).start()
 
     def activations(c):
         r, k = c // 4, c % 4
-        partial_recv(c).wait_recv()
+        for first, count in spans((c + 4) % 8):
+            partial_copy(c, c, first, count).wait_recv()
         full = pf[c] + pr[c].astype(F32)
         gate, up, dh = full[:, 0:128], full[:, 128:256], full[:, 256:384]
         sig = jax.nn.sigmoid(gate)
@@ -299,13 +306,16 @@
                 forward(r, s, way).wait_recv()
                 hand(r, s // 2, way).start()
 
+    def rows_done(r, s):
+        for way in range(2):
+            if handed(r, s):
+                hand(r, s // 2, way).wait_recv()
+            elif (r, s // 2) not in HANDED:
+                forward(r, s, way).wait_recv()
+
     def chunk_done(r, j):
-        for way in range(2):
-            if (r, j) in HANDED:
-                hand(r, j, way).wait_recv()
-            else:
-                forward(r, 2 * j, way).wait_recv()
-                forward(r, 2 * j + 1, way).wait_recv()
+        rows_done(r, 2 * j)
+        rows_done(r, 2 * j + 1)
         products(r * 4 + j)
         if r == 1:
             activations(4 + j)
@@ -426,51 +436,55 @@
         local.start()
 
     pending = []
-    for i in range(len(steps)):
-        r, s = steps[i]
-        if i > 0:
-            arrive(i)
-        if i == CROSS_AT:
-            cross.wait_recv()
-        issue_z(i)
-        if i >= 1:
-            forward_step(i - 1)
-        if i >= 2:
-            hand_step(i - 2)
-        if s % 2 == 1:
-            pending.append((i + (3 if (r, s // 2) in HANDED else 2), r, s // 2))
-        while pending and pending[0][0] <= i:
-            _, r, j = pending.pop(0)
-            chunk_done(r, j)
-    forward_step(15)
-    hand_step(14)
+    for i in range(len(steps) + LAG):
+        if i < len(steps):
+            r, s = steps[i]
+            if i > 0:
+                arrive(i)
+            if i == CROSS_AT:
+                cross.wait_recv()
+            issue_z(i)
+            if s % 2 == 1:
+                pending.append((i + LAG + (2 if (r, s // 2) in HANDED else 1), r, s // 2))
+        if i >= LAG:
+            forward_step(i - LAG)
+        if i >= LAG + 1:
+            hand_step(i - LAG - 1)
+        while len(pending) > 1 and pending[0][0] <= i:
+            chunk_done(*pending.pop(0)[1:])
+    final = ready[3]
     parts(ready[0])
     while len(pending) > 1:
         chunk_done(*pending.pop(0)[1:])
     parts(ready[1])
-    chunk_done(*pending.pop(0)[1:])
+    rows_done(1, 2 * final)
+    products(4 + final, 0, 64)
+    rows_done(1, 2 * final + 1)
+    products(4 + final, 64, 64)
+    activations(4 + final)
+    activations(ready[2])
+    parts(ready[2])
     nears(ready[0])
-    activations(ready[3])
+    activations(final)
+    parts(final)
     grads(0)
-    parts(ready[2])
     nears(ready[1])
     grads(1)
-    sums(ready[0])
-    parts(ready[3])
     nears(ready[2])
     grads(2)
+    sums(ready[0])
+    nears(final)
+    grads(3)
     sums(ready[1])
+    grads(4)
     gather_home(ready[0])
-    nears(ready[3])
-    grads(3)
-    grads(4)
     sums(ready[2])
+    grads(5)
     gather_home(ready[1])
-    grads(5)
     grads(6)
-    sums(ready[3])
+    sums(final)
     gather_home(ready[2])
-    gather_home(ready[3])
+    gather_home(final)
 
     for n in range(n_cols):
         for j in range(3):
@@ -490,7 +504,8 @@
             if s % 2 == 0 and (r, s // 2) in HANDED:
                 hand(r, s // 2, way).wait_send()
     for c in range(8):
-        partial_send(c).wait_send()
+        for first, count in spans(c):
+            partial_send(c, first, count).wait_send()
     for g in range(4):
         for way in range(2):
             anti_send(g, way).wait_send()
@@ -568,8 +583,8 @@
             dma((2, 2, NZ)),
             dma((2, 2, NZ)),
             dma((2, 2, NZ)),
-            dma((8,)),
-            dma((8,)),
+            dma((8, 2)),
+            dma((8, 2)),
             dma((2,)),
             dma((4,)),
             dma((4,)),

time: 123 us -> 122 us (level)
  no operation moved by 1% of the time
where the time goes in v3:
time: 122 us
  Pallas kernels  122 us (100%)
    pallas_call x1, Pallas kernels, body(): pl.pallas_call(kernel, out_shape=(jax.ShapeDtypeStruct((EF, CAP, width),...  117 us
    pallas_call x1, Pallas kernels, body(): pl.pallas_call(finish, grid=(width // block,), out_shape=(jax.ShapeDtypeS...  4.06 us

profile of v3, /device:TPU:1, one launch (start us, length us, event | category | flops | bytes accessed | tf_op | source)
XLA Modules:
  0.0 122.2 jit_solution(16656365604739191716)
XLA Ops:
  0.6 117.5 %shard_map.102 = (bf16[4,16,3584]{2,1,0:T(8,128)(2,1)}, bf16[256,128]{1,0:T(8,128)(2,1)}, bf16[3584,128]{1,0:T(8,128)(2,1)}, bf16[3584,128]{1,0:T(8,128)(2,1)}, bf16[128,3584]{1,0:T(8,128)(2,1)}) custom-call(s32[8,256]{1,0:T(8,128)} %bitcast.22, f32[8,256]{1,0:T(8,128)} %bitcast.23, bf16[256,3584]{1,0:T(8,128)(2,1)} %bitcast.16, bf16[256,3584]{1,0:T(8,128)(2,1)} %bitcast.17, ...), custom_call_target="tpu_custom_call" | custom-call | tf_op jit(solution)/shard_map/pallas_call | solution.py:536
  118.1 4.1 %shard_map.103 = (bf16[256,3584]{1,0:T(8,128)(2,1)}, bf16[3584,128]{1,0:T(8,128)(2,1)}, bf16[3584,128]{1,0:T(8,128)(2,1)}, bf16[128,3584]{1,0:T(8,128)(2,1)}) custom-call(bf16[64,3584]{1,0:T(8,128)(2,1)} %bitcast.21, bf16[256,128]{1,0:T(8,128)(2,1)} %get-tuple-element.14.pmat_t, bf16[3584,128]{1,0:T(8,128)(2,1)} %get-tuple-element.15.gate, ...), custom_call_target="tpu_custom_call" | custom-call | tf_op jit(solution)/shard_map/pallas_call | solution.py:616
